TPU v7x, 32 devices: a whole 2x2x4 slice. The times are simulated.
32 devices in a mesh: mem: 4 (over y, x), lon: 8 (over z, core).
Axes of the slice: x: 2, y: 2, z: 4, core: 2. Of those that a mesh axis runs over, the one named last changes fastest.
Arguments:
- members: float32 [16, 256, 12, 720], P('mem', 'lon'), may hold values from -6 to 6
- control: float32 [256, 12, 720], P('lon', None, 'mem'), may hold values from -6 to 6
- sea_mask: int32 [256, 12], P('lon'), may hold values 0 or 1
- depth_class: int32 [256, 12], P('lon'), may hold values from 0 to 3
- wind_dir: int32 [256, 12], P('lon'), may hold values from 0 to 23
- growth: float32 [30], replicated, may hold values from 0.2 to 2
- kernel: float32 [720, 720], replicated, may hold values from -0.21875 to 0.21875
Outputs:
- spectra: float32 [16, 256, 12, 720], P('mem', 'lon')
All inputs are finite; a program needn't handle non-finite values. No bound on the sum of `sea_mask` on one device may be relied on, other than what follows from the above.
Results may differ from a plain program's by a relative error of at most 0.0001.
Values sent between devices are 32-bit elements; how exact they have to be, the bound alone decides.
A program may use at most 128 MiB of HBM per device.

v0:
```python
import math

import jax
import jax.numpy as jnp
from jax import lax
from jax.sharding import PartitionSpec as P

DIRS = 24
FREQS = 30


def extended(x, sides, width):
    for axis, dim in sides:
        count, length = (lax.axis_size(axis), x.shape[dim])
        up = [(i, (i + 1) % count) for i in range(count)]
        down = [(j, i) for i, j in up]
        last = lax.slice_in_dim(x, length - width, length, axis=dim)
        initial = lax.slice_in_dim(x, 0, width, axis=dim)
        before = lax.ppermute(last, axis, up)
        after = lax.ppermute(initial, axis, down)
        x = jnp.concatenate([before, x, after], axis=dim)
    return x


def wave_tables(sea_mask, depth_class, wind_dir, growth):
    cells_lon, rows_lat = sea_mask.shape
    frequency = 0.04 * jnp.power(jnp.float32(1.1), jnp.arange(FREQS).astype(jnp.float32))
    deep_speed = 9.81 / (4.0 * math.pi * frequency)
    depths = jnp.array([10.0, 30.0, 80.0, 200.0], jnp.float32)
    shallow = jnp.sqrt(9.81 * depths)
    group_speed = jnp.minimum(deep_speed[None, :], shallow[:, None])
    fastest = 9.81 / (4.0 * math.pi * 0.04)
    onehot = (depth_class[..., None] == jnp.arange(4)).astype(jnp.float32)
    cell_speed = 0.7 * jnp.sum(onehot[..., None] * group_speed, axis=2) / fastest
    angles = 2.0 * math.pi * jnp.arange(DIRS).astype(jnp.float32) / DIRS
    zonal_speed = (cell_speed[:, :, None, :] * jnp.cos(angles)[:, None]).reshape(
        cells_lon, rows_lat, DIRS * FREQS
    )
    merid_speed = (cell_speed[:, :, None, :] * jnp.sin(angles)[:, None]).reshape(
        cells_lon, rows_lat, DIRS * FREQS
    )
    relative = (jnp.arange(DIRS)[None, None, :] - wind_dir[..., None]).astype(jnp.float32)
    alignment = jnp.maximum(jnp.cos(2.0 * math.pi * relative / DIRS), 0.0)
    wind_gain = (alignment[..., None] * growth[None, None, None, :]).reshape(
        cells_lon, rows_lat, DIRS * FREQS
    )
    ocean = sea_mask.astype(jnp.float32)[..., None]
    return (zonal_speed, merid_speed, wind_gain, ocean)


def advect(centre, west_side, east_side, zonal_speed, merid_speed):
    lat_pad = jnp.pad(centre, ((0, 0), (0, 0), (1, 1), (0, 0)))
    south_side = lat_pad[:, :, :-2]
    north_side = lat_pad[:, :, 2:]
    flux = jnp.maximum(zonal_speed, 0.0) * (centre - west_side) + jnp.minimum(zonal_speed, 0.0) * (
        east_side - centre
    )
    flux = (
        flux
        + jnp.maximum(merid_speed, 0.0) * (centre - south_side)
        + jnp.minimum(merid_speed, 0.0) * (north_side - centre)
    )
    return centre - flux


def source(field, wind_gain, ocean, kernel):
    energy = jnp.mean(field * field, axis=-1, keepdims=True)
    shape = field.shape
    transfer = jnp.dot(
        field.reshape(-1, shape[-1]),
        kernel,
        precision=lax.Precision.HIGHEST,
        preferred_element_type=jnp.float32,
    ).reshape(shape)
    return (field + 0.1 * (wind_gain * field - 0.5 * energy * field + transfer)) * ocean


def padded_step(padded, tables, kernel):
    zonal_speed, merid_speed, wind_gain, ocean = tables
    moved = advect(padded[:, 1:-1], padded[:, :-2], padded[:, 2:], zonal_speed, merid_speed)
    return source(moved, wind_gain, ocean, kernel)


def thin_step(field, tables, kernel):
    padded = extended(field, (("lon", 1),), 1)
    return padded_step(padded, tables, kernel)


def shards(members, control, sea_mask, depth_class, wind_dir, growth, kernel):
    member_count = members.shape[0] * lax.axis_size("mem")
    local_total = jnp.sum(members, axis=0)
    tables = wave_tables(sea_mask, depth_class, wind_dir, growth)
    ocean = tables[3]
    member_total = lax.psum(local_total, "mem")
    control_full = lax.all_gather(control, "mem", axis=2, tiled=True)
    field = (members - member_total / member_count + control_full) * ocean
    field = thin_step(field, tables, kernel)
    field = thin_step(field, tables, kernel)
    return field


def solution(mesh):
    return jax.shard_map(
        shards,
        mesh=mesh,
        in_specs=(
            P("mem", "lon", None, None),
            P("lon", None, "mem"),
            P("lon", None),
            P("lon", None),
            P("lon", None),
            P(),
            P(),
        ),
        out_specs=P("mem", "lon", None, None),
        check_vma=False,
    )
```

profile of v0, /device:TPU:0, one launch (start us, length us, event | category | flops | bytes accessed | tf_op | source)
XLA Modules:
  0.0 206.2 jit_solution(917678572837277976)
XLA Ops:
  6.6 4.0 %reduce_sum.36 = f32[32,12,720]{2,0,1:T(8,128)} reduce(f32[4,32,12,720]{3,1,2,0:T(8,128)} %param.8, f32[]{:T(128)} %constant.14.clone.1), dimensions={0}, to_apply=%region_0.0 | reduce | flops 829440 | bytes 5529604 | tf_op jit(solution)/shard_map/reduce_sum | solution.py:91
  10.7 2.0 copy.14
  13.4 0.5 multiply_reduce_fusion.2
  14.1 0.7 cosine_maximum_fusion
  14.8 3.2 %mul.268 = f32[32,12,24,30]{3,2,0,1:T(8,128)} broadcast(f32[32,12,24]{2,0,1:T(8,128)S(1)} %cosine_maximum_fusion), dimensions={0,1,2} | broadcast | bytes 1142784 | tf_op jit(solution)/shard_map/mul | solution.py:44
  18.1 4.9 %mul.269 = f32[32,12,720]{2,0,1:T(8,128)} reshape(f32[32,12,24,30]{3,2,0,1:T(8,128)} %mul.268) | data formatting | bytes 2211840 | tf_op jit(solution)/shard_map/mul | solution.py:44
  22.9 2.5 %mul.250 = f32[32,12,24,30]{3,2,0,1:T(8,128)} broadcast(f32[32,12,30]{2,0,1:T(8,128)S(1)} %copy.16), dimensions={0,1,3} | broadcast | bytes 1152000 | tf_op jit(solution)/shard_map/mul | solution.py:36
  25.4 4.6 %mul.251 = f32[32,12,720]{2,0,1:T(8,128)} reshape(f32[32,12,24,30]{3,2,0,1:T(8,128)} %mul.250) | data formatting | bytes 2211840 | tf_op jit(solution)/shard_map/mul | solution.py:36
  30.0 3.3 %multiply_maximum_fusion.1 = (f32[32,12,720]{2,0,1:T(8,128)S(1)}, f32[32,12,720]{2,0,1:T(8,128)}, f32[32,12,720]{2,0,1:T(8,128)}, f32[32,12,720]{2,0,1:T(8,128)}) fusion(f32[32,12,720]{2,0,1:T(8,128)} %mul.251, f32[720]{0:T(1024)S(1)} %mul.253, f32[720]{0:T(1024)S(1)} %mul.261), kind=kLoop, calls=%fused_computation.44 | loop fusion | flops 1658880 | bytes 5535360 | tf_op jit(solution)/shard_map/max | solution.py:55
  33.3 34.7 %all-reduce.4.cloned.1.call-done = f32[32,12,720]{2,0,1:T(8,128)} async-done(((f32[32,12,720]{2,0,1:T(8,128)}), f32[32,12,720]{2,0,1:T(8,128)}) %all-reduce.4.cloned.1.call-update) | async-done | bytes 1105936 | tf_op jit(solution)/shard_map/psum | solution.py:94
  68.0 2.4 %broadcast_multiply_fusion.1 = f32[32,12,720]{2,0,1:T(8,128)} fusion(f32[32,12,720]{2,0,1:T(8,128)} %all-reduce.4.cloned.1.call-done), kind=kLoop, calls=%fused_computation.47 | loop fusion | flops 276480 | bytes 2211840 | tf_op jit(solution)/shard_map/div | solution.py:96
  70.4 66.5 %all-gather.2.cloned.1.call-done = f32[32,12,720]{0,1,2:T(8,128)} async-done(((f32[32,12,180]{0,1,2:T(8,128)}), f32[32,12,720]{0,1,2:T(8,128)}) %all-gather.2.cloned.1.call-update) | async-done | bytes 1105936 | tf_op jit(solution)/shard_map/all_gather | solution.py:95
  136.9 5.4 %copy.15 = f32[32,12,720]{2,0,1:T(8,128)} copy(f32[32,12,720]{0,1,2:T(8,128)} %all-gather.2.cloned.1.call-done) | data formatting | bytes 2211840 | tf_op jit(solution)/shard_map/all_gather | solution.py:95
  142.3 4.1 %add_multiply_fusion.2 = f32[4,32,12,720]{3,1,2,0:T(8,128)S(1)} fusion(f32[4,32,12,720]{3,1,2,0:T(8,128)} %param.8, f32[32,12]{0,1:T(8,128)S(1)} %convert_element_type.39, f32[32,12,720]{2,0,1:T(8,128)} %copy.15, f32[32,12,720]{2,0,1:T(8,128)} %broadcast_multiply_fusion.1), kind=kLoop, calls=%fused_computation.36 | loop fusion | flops 3317760 | bytes 11060736 | tf_op jit(solution)/shard_map/mul | solution.py:96
  146.6 3.5 %collective-permute-start.1 = (f32[4,1,12,720]{3,1,2,0:T(1,128)S(1)}, f32[4,1,12,720]{3,1,2,0:T(1,128)S(1)}, u32[]{:S(2)}, u32[]{:S(2)}) collective-permute-start(f32[4,1,12,720]{3,1,2,0:T(1,128)S(1)} %get-tuple-element.12), channel_id=1, source_target_pairs={{1,0},{2,1},{3,2},{4,3},{5,4},{6,5},{7,6},{0,7},{9,8},{10,9},{11,1... | collective-permute-start | bytes 414728 | tf_op jit(solution)/shard_map/ppermute | solution.py:20
  150.3 2.9 %collective-permute-done = f32[4,1,12,720]{3,1,2,0:T(1,128)S(1)} collective-permute-done((f32[4,1,12,720]{3,1,2,0:T(1,128)S(1)}, f32[4,1,12,720]{3,1,2,0:T(1,128)S(1)}, u32[]{:S(2)}, u32[]{:S(2)}) %collective-permute-start) | collective-permute-done | bytes 138272 | tf_op jit(solution)/shard_map/ppermute | solution.py:19
  153.2 4.5 %multiply_reduce_fusion.1 = (f32[4,32,12]{1,2,0:T(8,128)S(1)}, f32[4,32,12,720]{3,1,2,0:T(8,128)S(1)}) fusion(f32[4,32,12,720]{3,1,2,0:T(8,128)S(1)} %add_multiply_fusion.2, f32[32,12,720]{2,0,1:T(8,128)S(1)} %copy-done.2, f32[32,12,720]{2,0,1:T(8,128)S(1)} %copy-done.3, f32[4,1,12,720]{3,1,2,0:T(1,128)S(1)} %collective-permute-done.1, ...), kind=kLoop, calls=%fused_computation.35 | loop fusion | flops 17693184 | bytes 13553664 | tf_op jit(solution)/shard_map/reduce_sum | solution.py:67
  157.7 14.8 %add_multiply_fusion.1 = f32[4,32,12,720]{3,1,2,0:T(8,128)S(1)} fusion(f32[4,32,12,720]{3,1,2,0:T(8,128)S(1)} %get-tuple-element.8, f32[4,32,12]{1,2,0:T(8,128)S(1)} %broadcast_multiply_fusion.4, f32[32,12,720]{2,0,1:T(8,128)S(1)} %broadcast_multiply_fusion, f32[32,12]{0,1:T(8,128)S(1)} %convert_element_type.39, f32[720,720]{1,0:T(8,128)S(1)} %copy-done), kind=kOutput, calls=%fused_computation.34 | convolution fusion | flops 9562890240 | bytes 12034560 | tf_op jit(solution)/shard_map/dot_general | solution.py:69
  172.5 0.2 fusion.37
  172.7 1.3 collective-permute-start.2
  174.0 2.3 %collective-permute-start.3 = (f32[4,1,12,720]{3,1,2,0:T(1,128)S(1)}, f32[4,1,12,720]{3,1,2,0:T(1,128)S(1)}, u32[]{:S(2)}, u32[]{:S(2)}) collective-permute-start(f32[4,1,12,720]{3,1,2,0:T(1,128)S(1)} %get-tuple-element.10), channel_id=1, source_target_pairs={{1,0},{2,1},{3,2},{4,3},{5,4},{6,5},{7,6},{0,7},{9,8},{10,9},{11,1... | collective-permute-start | bytes 414728 | tf_op jit(solution)/shard_map/ppermute | solution.py:20
  176.3 4.0 %collective-permute-done.2 = f32[4,1,12,720]{3,1,2,0:T(1,128)S(1)} collective-permute-done((f32[4,1,12,720]{3,1,2,0:T(1,128)S(1)}, f32[4,1,12,720]{3,1,2,0:T(1,128)S(1)}, u32[]{:S(2)}, u32[]{:S(2)}) %collective-permute-start.2) | collective-permute-done | bytes 138272 | tf_op jit(solution)/shard_map/ppermute | solution.py:19
  180.3 4.3 %multiply_reduce_fusion = (f32[4,32,12]{1,2,0:T(8,128)S(1)}, f32[4,32,12,720]{3,1,2,0:T(8,128)S(1)}) fusion(f32[4,32,12,720]{3,1,2,0:T(8,128)S(1)} %add_multiply_fusion.1, f32[32,12,720]{2,0,1:T(8,128)S(1)} %copy-done.2, f32[32,12,720]{2,0,1:T(8,128)S(1)} %copy-done.3, f32[4,1,12,720]{3,1,2,0:T(1,128)S(1)} %collective-permute-done.3, ...), kind=kLoop, calls=%fused_computation.33 | loop fusion | flops 17693184 | bytes 13553664 | tf_op jit(solution)/shard_map/reduce_sum | solution.py:67
  184.6 14.8 %add_multiply_fusion = f32[4,32,12,720]{3,1,2,0:T(8,128)} fusion(f32[4,32,12,720]{3,1,2,0:T(8,128)S(1)} %get-tuple-element.6, f32[4,32,12]{1,2,0:T(8,128)S(1)} %broadcast_multiply_fusion.3, f32[32,12,720]{2,0,1:T(8,128)S(1)} %broadcast_multiply_fusion, f32[32,12]{0,1:T(8,128)S(1)} %convert_element_type.39, f32[720,720]{1,0:T(8,128)S(1)} %copy-done), kind=kOutput, calls=%fused_computation.32 | convolution fusion | flops 9562890240 | bytes 12034560 | tf_op jit(solution)/shard_map/dot_general | solution.py:69
  (47 shorter events, 1.3 us)
Async XLA Ops:
  6.5 151.1 %copy-start = (f32[720,720]{1,0:T(8,128)S(1)}, f32[720,720]{1,0:T(8,128)}, u32[]{:S(2)}) copy-start(f32[720,720]{1,0:T(8,128)} %param.14) | copy-start | bytes 6220804
  6.5 6.7 %copy-start.10 = (f32[4]{0:T(128)S(1)}, f32[4]{0:T(128)}, u32[]{:S(2)}) copy-start(f32[4]{0:T(128)} %constant.49) | copy-start | bytes 52
  6.5 4.2 %copy-start.5 = (f32[32,12,180]{2,0,1:T(8,128)S(1)}, f32[32,12,180]{2,0,1:T(8,128)}, u32[]{:S(2)}) copy-start(f32[32,12,180]{2,0,1:T(8,128)} %param.9) | copy-start | bytes 829444
  6.5 6.3 %copy-start.7 = (s32[32,12]{0,1:T(8,128)S(1)}, s32[32,12]{0,1:T(8,128)}, u32[]{:S(2)}) copy-start(s32[32,12]{0,1:T(8,128)} %param.10) | copy-start | bytes 4612
  6.5 6.6 %copy-start.9 = (f32[30]{0:T(128)S(1)}, f32[30]{0:T(128)}, u32[]{:S(2)}) copy-start(f32[30]{0:T(128)} %param.13) | copy-start | bytes 364
  6.5 6.8 %copy-start.8 = (s32[32,12]{0,1:T(8,128)S(1)}, s32[32,12]{0,1:T(8,128)}, u32[]{:S(2)}) copy-start(s32[32,12]{0,1:T(8,128)} %param.11) | copy-start | bytes 4612
  6.6 7.6 %copy-start.6 = (s32[32,12]{0,1:T(8,128)S(1)}, s32[32,12]{0,1:T(8,128)}, u32[]{:S(2)}) copy-start(s32[32,12]{0,1:T(8,128)} %param.12) | copy-start | bytes 4612
  6.6 61.4 %all-reduce.4.cloned.1.call-start = ((), (), s32[]{:S(2)}) async-start(), calls=%async_computation | async-start | bytes 2359296 | tf_op jit(solution)/shard_map/psum | solution.py:94
  10.7 126.2 %all-gather.2.cloned.1.call-start = ((), (), s32[]{:S(2)}) async-start(), calls=%async_computation.1 | async-start | bytes 7372800 | tf_op jit(solution)/shard_map/all_gather | solution.py:95
  142.3 7.9 %copy-start.4 = (f32[32,12,720]{2,0,1:T(8,128)S(1)}, f32[32,12,720]{2,0,1:T(8,128)}, u32[]{:S(2)}) copy-start(f32[32,12,720]{2,0,1:T(8,128)} %mul.269) | copy-start | bytes 3317764
  142.3 10.9 %copy-start.1 = (f32[32,12,720]{2,0,1:T(8,128)S(1)}, f32[32,12,720]{2,0,1:T(8,128)}, u32[]{:S(2)}) copy-start(f32[32,12,720]{2,0,1:T(8,128)} %get-tuple-element.14) | copy-start | bytes 3317764
  142.3 10.9 %copy-start.2 = (f32[32,12,720]{2,0,1:T(8,128)S(1)}, f32[32,12,720]{2,0,1:T(8,128)}, u32[]{:S(2)}) copy-start(f32[32,12,720]{2,0,1:T(8,128)} %get-tuple-element.17) | copy-start | bytes 3317764
  142.3 10.9 %copy-start.3 = (f32[32,12,720]{2,0,1:T(8,128)S(1)}, f32[32,12,720]{2,0,1:T(8,128)}, u32[]{:S(2)}) copy-start(f32[32,12,720]{2,0,1:T(8,128)} %get-tuple-element.18) | copy-start | bytes 3317764
  146.6 6.6 %collective-permute-start = (f32[4,1,12,720]{3,1,2,0:T(1,128)S(1)}, f32[4,1,12,720]{3,1,2,0:T(1,128)S(1)}, u32[]{:S(2)}, u32[]{:S(2)}) collective-permute-start(f32[4,1,12,720]{3,1,2,0:T(1,128)S(1)} %get-tuple-element.11), channel_id=1, source_target_pairs={{0,1},{1,2},{2,3},{3,4},{4,5},{5,6},{6,7},{7,0},{8,9},{9,10},{10,1... | collective-permute-start | bytes 414728 | tf_op jit(solution)/shard_map/ppermute | solution.py:19
  146.6 6.5 %collective-permute-start.1 = (f32[4,1,12,720]{3,1,2,0:T(1,128)S(1)}, f32[4,1,12,720]{3,1,2,0:T(1,128)S(1)}, u32[]{:S(2)}, u32[]{:S(2)}) collective-permute-start(f32[4,1,12,720]{3,1,2,0:T(1,128)S(1)} %get-tuple-element.12), channel_id=1, source_target_pairs={{1,0},{2,1},{3,2},{4,3},{5,4},{6,5},{7,6},{0,7},{9,8},{10,9},{11,1... | collective-permute-start | bytes 414728 | tf_op jit(solution)/shard_map/ppermute | solution.py:20
  172.7 7.5 %collective-permute-start.2 = (f32[4,1,12,720]{3,1,2,0:T(1,128)S(1)}, f32[4,1,12,720]{3,1,2,0:T(1,128)S(1)}, u32[]{:S(2)}, u32[]{:S(2)}) collective-permute-start(f32[4,1,12,720]{3,1,2,0:T(1,128)S(1)} %get-tuple-element.9), channel_id=1, source_target_pairs={{0,1},{1,2},{2,3},{3,4},{4,5},{5,6},{6,7},{7,0},{8,9},{9,10},{10,1... | collective-permute-start | bytes 414728 | tf_op jit(solution)/shard_map/ppermute | solution.py:19
  174.0 6.3 %collective-permute-start.3 = (f32[4,1,12,720]{3,1,2,0:T(1,128)S(1)}, f32[4,1,12,720]{3,1,2,0:T(1,128)S(1)}, u32[]{:S(2)}, u32[]{:S(2)}) collective-permute-start(f32[4,1,12,720]{3,1,2,0:T(1,128)S(1)} %get-tuple-element.10), channel_id=1, source_target_pairs={{1,0},{2,1},{3,2},{4,3},{5,4},{6,5},{7,6},{0,7},{9,8},{10,9},{11,1... | collective-permute-start | bytes 414728 | tf_op jit(solution)/shard_map/ppermute | solution.py:20
Sparse Core Ops, SparseCore 0:
  10.8 57.1 all-reduce.3
  70.0 66.8 all-gather.1
where the time goes:
time: 207 us; the launch traced here: 206 us
  waiting for transfers between devices  108 us (52%)
  matrix products  29.6 us (14%)
  other arithmetic  24.1 us (12%)
  local copies, waits for them, and re-layouts  23.5 us (11%)
  between operations  13.6 us (7%)
  starting transfers between devices  7.26 us (4%)
    all_gather x1, waiting for transfers between devices, shards(): control_full = lax.all_gather(control, 'mem', axis=2, tiled=True)  66.5 us
    psum x1, waiting for transfers between devices, shards(): member_total = lax.psum(local_total, 'mem')  34.7 us
    dot_general x2, matrix products, source(): jnp.dot(field.reshape(-1, shape[-1]), kernel, precision=lax.Precision.HIG...  29.6 us
    reduce_sum x2, other arithmetic, source(): energy = jnp.mean(field * field, axis=-1, keepdims=True)  8.77 us
    mul x4, local copies, waits for them, and re-layouts, wave_tables(): alignment[..., None] * growth[None, None, None, :]  8.19 us
    mul x4, local copies, waits for them, and re-layouts, wave_tables(): cell_speed[:, :, None, :] * jnp.cos(angles)[:, None]  7.2 us
    ppermute x2, waiting for transfers between devices, extended(): before = lax.ppermute(last, axis, up)  6.83 us
    ppermute x2, starting transfers between devices, extended(): after = lax.ppermute(initial, axis, down)  5.86 us
  transfers between devices with their start and end apart: 6, of which 4 were waited for; matrix products, arithmetic and copies ran while one was open for 12% of the time, Pallas kernels for 0%

commit v1 on v0

v1 whole, which is shorter than its diff:
```python
import functools
import math

import jax
import jax.numpy as jnp
import numpy as np
from jax import lax
from jax.experimental import pallas as pl
from jax.experimental.pallas import tpu as pltpu
from jax.sharding import PartitionSpec as P

DIRS = 24
FREQS = 30
LANES = 128
CLASSES = 4


def round_up(x, to):
    return -(-x // to) * to


def constants(bins, width):
    frequency = 0.04 * 1.1 ** np.arange(FREQS, dtype=np.float64)
    deep = 9.81 / (4.0 * math.pi * frequency)
    shallow = np.sqrt(9.81 * np.array([10.0, 30.0, 80.0, 200.0]))
    speed = 0.7 * np.minimum(deep[None], shallow[:, None]) / (9.81 / (4.0 * math.pi * 0.04))
    angles = 2.0 * math.pi * np.arange(DIRS) / DIRS
    cos, sin = np.cos(angles), np.sin(angles)
    cos[np.abs(cos) < 1e-9] = 0.0
    sin[np.abs(sin) < 1e-9] = 0.0
    lift = lambda v: (v[None, :, None] * speed[:, None, :]).reshape(CLASSES, bins)
    a, b = lift(np.abs(cos)), lift(np.abs(sin))
    tab = np.zeros((LANES, 3 * width), np.float32)
    tab[:CLASSES, :bins] = a
    tab[:CLASSES, width : width + bins] = b
    tab[:CLASSES, 2 * width : 2 * width + bins] = -(a + b)
    tab[CLASSES + DIRS, 2 * width : 2 * width + bins] = 1.0
    rel = np.arange(DIRS)[None, :] - np.arange(DIRS)[:, None]
    align = np.maximum(np.cos(2.0 * math.pi * rel / DIRS), 0.0)
    wind = np.zeros((LANES, width), np.float32)
    wind[CLASSES : CLASSES + DIRS, :bins] = 0.1 * np.repeat(align, FREQS, axis=1)
    one = np.zeros((LANES, width), np.float32)
    one[CLASSES + DIRS, :bins] = 1.0
    cs = np.zeros(width, np.int32)
    sn = np.zeros(width, np.int32)
    cs[:bins] = np.repeat(np.sign(cos), FREQS)
    sn[:bins] = np.repeat(np.sign(sin), FREQS)
    return tab, wind, one, cs, sn


def spans(sign):
    out = []
    for c in range(len(sign) // LANES):
        s = sign[c * LANES : (c + 1) * LANES]
        if (s >= 0).all():
            out.append(1)
        elif (s <= 0).all():
            out.append(-1)
        else:
            pos = np.nonzero(s > 0)[0]
            out.append((int(pos[0]), int(pos[-1]) + 1))
            assert (s[pos[0] : pos[-1] + 1] >= 0).all()
    return out


def kernel(
    n, lons, count, rows_lat, tile, bins, width, zspan, mspan, total_members,
    m_hbm, ctrl_hbm, k_hbm, oh_ref, tab_ref, wind_ref, one_ref, growth_ref,
    out_hbm,
    mv, ctrlv, kv, ctrlp, dl, rsb, dfull, f0, f1, ta, tb, tc, tw, rk, lhs, gbuf, ebuf,
    snd, rcv,
    m_sem, in_sem, out_sem, rs_s, rs_r, ag_s, ag_r, h_s, h_r,
):
    me = lax.axis_index("mem")
    at = lax.axis_index("lon")
    right = lax.rem(at + 1, lons)
    left = lax.rem(at + lons - 1, lons)
    cells = rows_lat * tile
    part = cells // n
    cols = width // LANES
    block = 3 if rows_lat % 3 == 0 else 1
    blocks = rows_lat // block
    own_bins = ctrlv.shape[1]

    def peer(o):
        return lax.rem(me + o, n)

    def rows_of(q):
        return pl.ds(pl.multiple_of(q * part, 8), part)

    def m_copy(o):
        r = rows_of(peer(o))
        return pltpu.make_async_copy(m_hbm.at[:, r], mv.at[:, r], m_sem.at[o])

    order = list(range(1, n)) + [0]
    c_copy = pltpu.make_async_copy(ctrl_hbm, ctrlv, in_sem.at[0])
    k_copy = pltpu.make_async_copy(k_hbm, kv, in_sem.at[1])
    c_copy.start()
    for o in order:
        m_copy(o).start()
    k_copy.start()

    barrier = pltpu.get_barrier_semaphore()
    for o in range(1, n):
        pl.semaphore_signal(barrier, inc=1, device_id={"mem": peer(o)}, device_id_type=pl.DeviceIdType.MESH)
    for side in (left, right):
        pl.semaphore_signal(barrier, inc=1, device_id={"lon": side}, device_id_type=pl.DeviceIdType.MESH)

    ctrlp[...] = jnp.zeros_like(ctrlp)
    c_copy.wait()
    for k in range(n):
        @pl.when(me == k)
        def _():
            ctrlp[:, k * own_bins : (k + 1) * own_bins] = ctrlv[...]

    pl.semaphore_wait(barrier, n + 1)

    def rs_copy(o):
        q = peer(o)
        return pltpu.make_async_remote_copy(
            src_ref=dl.at[rows_of(q)], dst_ref=rsb.at[o - 1], send_sem=rs_s.at[o - 1], recv_sem=rs_r.at[o - 1],
            device_id={"mem": q}, device_id_type=pl.DeviceIdType.MESH,
        )

    def ag_copy(o):
        r = rows_of(me)
        return pltpu.make_async_remote_copy(
            src_ref=dfull.at[r], dst_ref=dfull.at[r], send_sem=ag_s.at[o - 1], recv_sem=ag_r.at[o - 1],
            device_id={"mem": peer(o)}, device_id_type=pl.DeviceIdType.MESH,
        )

    def ag_arrival(o):
        r = rows_of(lax.rem(me + n - o, n))
        return pltpu.make_async_remote_copy(
            src_ref=dfull.at[r], dst_ref=dfull.at[r], send_sem=ag_s.at[o - 1], recv_sem=ag_r.at[o - 1],
            device_id={"mem": peer(o)}, device_id_type=pl.DeviceIdType.MESH,
        )

    step = 16 if part % 16 == 0 else 8
    for o in order:
        m_copy(o).wait()
        base = peer(o) * part

        @pl.loop(0, part // step)
        def _(i):
            r = pl.ds(pl.multiple_of(base + i * step, 8), step)
            s = mv[0, r, :]
            for m in range(1, count):
                s = s + mv[m, r, :]
            dl[r, :] = ctrlp[r, :] - s * (1.0 / total_members)

        if o:
            rs_copy(o).start()

    @pl.loop(0, rows_lat)
    def _(i):
        r = pl.ds(pl.multiple_of(i * tile, 8), tile)
        oh = oh_ref[r, :]
        hot = functools.partial(jnp.dot, oh, precision=lax.Precision.HIGHEST, preferred_element_type=jnp.float32)
        ta[r, :] = hot(tab_ref[:, :width])
        tb[r, :] = hot(tab_ref[:, width : 2 * width])
        tc[r, :] = hot(tab_ref[:, 2 * width :])
        tw[r, :] = hot(wind_ref[...] * growth_ref[...] + one_ref[...])

    rk[...] = jnp.zeros_like(rk)
    k_copy.wait()

    @pl.loop(0, bins // 16)
    def _(i):
        k = kv[pl.ds(pl.multiple_of(i * 16, 16), 16), :] * 0.1
        hi = k.astype(jnp.bfloat16)
        lo = (k - hi.astype(jnp.float32)).astype(jnp.bfloat16)
        rk[pl.ds(pl.multiple_of(i * 16, 16), 16), :bins] = hi
        rk[pl.ds(pl.multiple_of(width + i * 16, 16), 16), :bins] = hi
        rk[pl.ds(pl.multiple_of(2 * width + i * 16, 16), 16), :bins] = lo

    zero = jnp.zeros((tile, width), jnp.float32)
    for m in range(count):
        for f in (f0, f1):
            f[m, 0] = zero
            f[m, rows_lat + 1] = zero

        @pl.loop(0, rows_lat)
        def _(i):
            f0[m, i + 1, :, width - LANES :] = jnp.zeros((tile, LANES), jnp.float32)

    def halo_copies(sub, g):
        r = pl.ds(g * block, block)
        made = []
        for side, to in ((0, right), (1, left)):
            made.append(pltpu.make_async_remote_copy(
                src_ref=snd.at[sub, side, r], dst_ref=rcv.at[sub, side, r],
                send_sem=h_s.at[sub, side, g], recv_sem=h_r.at[sub, side, g],
                device_id={"lon": to}, device_id_type=pl.DeviceIdType.MESH,
            ))
        return made

    def keep_edges(sub, f, lat):
        snd[sub, 0, lat] = jnp.concatenate([f[m, lat + 1, tile - 1 : tile, :] for m in range(count)], axis=0)
        snd[sub, 1, lat] = jnp.concatenate([f[m, lat + 1, 0:1, :] for m in range(count)], axis=0)

    for o in range(1, n):
        rs_copy(o).wait_recv()

    @pl.loop(0, part // step)
    def _(i):
        r = pl.ds(pl.multiple_of(me * part + i * step, 8), step)
        s = dl[r, :]
        for o in range(1, n):
            s = s + rsb[o - 1, pl.ds(pl.multiple_of(i * step, 8), step), :]
        dfull[r, :] = s

    for o in range(1, n):
        ag_copy(o).start()

    def recentre(g):
        @pl.loop(0, block)
        def _(i):
            lat = g * block + i
            r = pl.ds(pl.multiple_of(lat * tile, 8), tile)
            sea = oh_ref[r, CLASSES + DIRS : CLASSES + DIRS + 1] > 0.5
            d = dfull[r, :]
            for m in range(count):
                f0[m, lat + 1, :, :bins] = jnp.where(sea, mv[m, r, :] + d, 0.0)
            keep_edges(0, f0, lat)
        for c in halo_copies(0, g):
            c.start()

    if blocks == n:
        for o in range(n):
            if o:
                ag_arrival(o).wait_recv()
            recentre(lax.rem(me + n - o, n))
    else:
        for o in range(1, n):
            ag_arrival(o).wait_recv()
        for g in range(blocks):
            recentre(g)

    row = lax.broadcasted_iota(jnp.int32, (tile, LANES), 0)
    lane = lax.broadcasted_iota(jnp.int32, (tile, LANES), 1)

    def pick(span, behind, ahead):
        if span == 1:
            return behind()
        if span == -1:
            return ahead()
        return jnp.where((lane >= span[0]) & (lane < span[1]), behind(), ahead())

    def substep(sub, f, write):
        @pl.loop(0, blocks)
        def _(g):
            for c in halo_copies(sub, g):
                c.wait_recv()

            @pl.loop(0, block)
            def _(i):
                lat = g * block + i
                r = pl.ds(pl.multiple_of(lat * tile, 8), tile)
                acc = [None] * count
                for c in range(cols):
                    l = slice(c * LANES, (c + 1) * LANES)
                    va, vb, vc = ta[r, l], tb[r, l], tc[r, l]
                    for m in range(count):
                        x = f[m, lat + 1, :, l]
                        west = lambda: jnp.where(row == 0, rcv[sub, 0, lat, m : m + 1, l], pltpu.roll(x, 1, 0))
                        east = lambda: jnp.where(row == tile - 1, rcv[sub, 1, lat, m : m + 1, l], pltpu.roll(x, tile - 1, 0))
                        south = lambda: f[m, lat, :, l]
                        north = lambda: f[m, lat + 2, :, l]
                        v = vc * x + va * pick(zspan[c], west, east) + vb * pick(mspan[c], south, north)
                        acc[m] = v * v if c == 0 else acc[m] + v * v
                        q = pl.ds(pl.multiple_of((i * count + m) * tile, 16), tile)
                        gbuf[q, l] = v
                        hi = v.astype(jnp.bfloat16)
                        lhs[q, l] = hi
                        lhs[q, width + c * LANES : width + (c + 1) * LANES] = (v - hi.astype(jnp.float32)).astype(jnp.bfloat16)
                for m in range(count):
                    q = pl.ds(pl.multiple_of((i * count + m) * tile, 16), tile)
                    e = jnp.sum(acc[m], axis=1, keepdims=True) * (0.05 / bins)
                    ebuf[q, :] = jnp.broadcast_to(e, (tile, LANES))

            chunk = 2 * LANES
            for c in range(0, width, chunk):
                l = slice(c, c + chunk)
                left_side = jnp.concatenate([lhs[...], lhs[:, :width]], axis=1)
                t = jnp.dot(left_side, rk[:, l], preferred_element_type=jnp.float32)
                for i in range(block):
                    lat = g * block + i
                    w = tw[pl.ds(pl.multiple_of(lat * tile, 8), tile), l]
                    for m in range(count):
                        k = (i * count + m) * tile
                        e = ebuf[k : k + tile, :]
                        e = jnp.concatenate([e] * (chunk // LANES), axis=1)
                        write(m, lat, l, gbuf[k : k + tile, l] * (w - e) + t[k : k + tile])
            if sub == 0:
                for i in range(block):
                    keep_edges(1, f1, g * block + i)
                for c in halo_copies(1, g):
                    c.start()
            else:
                out_copy(g).start()

    def out_copy(g):
        r = pl.ds(pl.multiple_of(g * block * tile, 8), block * tile)
        return pltpu.make_async_copy(mv.at[:, r], out_hbm.at[:, r], out_sem.at[g])

    def to_f1(m, lat, l, v):
        f1[m, lat + 1, :, l] = v

    def to_out(m, lat, l, v):
        stop = min(l.stop, bins)
        mv[m, pl.ds(pl.multiple_of(lat * tile, 8), tile), l.start : stop] = v[:, : stop - l.start]

    substep(0, f0, to_f1)
    substep(1, f1, to_out)

    for o in range(1, n):
        rs_copy(o).wait_send()
        ag_copy(o).wait_send()

    @pl.loop(0, blocks)
    def _(g):
        for sub in range(2):
            for c in halo_copies(sub, g):
                c.wait_send()
        out_copy(g).wait()


def shards(members, control, sea_mask, depth_class, wind_dir, growth, rate_kernel):
    count, tile, rows_lat, bins = members.shape
    n, lons = lax.axis_size("mem"), lax.axis_size("lon")
    cells = rows_lat * tile
    width = round_up(bins, 2 * LANES)
    part = cells // n
    block = 3 if rows_lat % 3 == 0 else 1
    blocks = rows_lat // block
    tab, wind, one, cs, sn = constants(bins, width)

    m = members.transpose(0, 2, 1, 3).reshape(count, cells, bins)
    c = control.transpose(1, 0, 2).reshape(cells, control.shape[2])
    flat = lambda x: x.T.reshape(cells, 1)
    sea, depth, wdir = flat(sea_mask), flat(depth_class), flat(wind_dir)
    slot = jnp.arange(LANES)[None, :]
    hot = (slot == depth) | (slot == wdir + CLASSES) | (slot == CLASSES + DIRS)
    hot = jnp.where(hot & (sea != 0), 1.0, 0.0).astype(jnp.float32)
    spread = jnp.pad(jnp.tile(growth, DIRS), (0, width - bins))[None]

    f32, bf16 = jnp.float32, jnp.bfloat16
    vmem = pl.BlockSpec(memory_space=pltpu.VMEM)
    hbm = pl.BlockSpec(memory_space=pl.ANY)
    field = pltpu.VMEM((count, rows_lat + 2, tile, width), f32)
    table = pltpu.VMEM((cells, width), f32)
    rows = block * count * tile
    out = pl.pallas_call(
        functools.partial(
            kernel, n, lons, count, rows_lat, tile, bins, width, spans(cs), spans(sn), count * n,
        ),
        out_shape=jax.ShapeDtypeStruct((count, cells, bins), f32),
        in_specs=[hbm, hbm, hbm] + [vmem] * 5,
        out_specs=hbm,
        scratch_shapes=[
            pltpu.VMEM((count, cells, bins), f32),
            pltpu.VMEM((cells, control.shape[2]), f32),
            pltpu.VMEM((bins, bins), f32),
            pltpu.VMEM((cells, bins), f32),
            pltpu.VMEM((cells, bins), f32),
            pltpu.VMEM((n - 1, part, bins), f32),
            pltpu.VMEM((cells, bins), f32),
            field, field, table, table, table, table,
            pltpu.VMEM((3 * width, width), bf16),
            pltpu.VMEM((rows, 2 * width), bf16),
            pltpu.VMEM((rows, width), f32),
            pltpu.VMEM((rows, LANES), f32),
            pltpu.VMEM((2, 2, rows_lat, count, width), f32),
            pltpu.VMEM((2, 2, rows_lat, count, width), f32),
            pltpu.SemaphoreType.DMA((n,)),
            pltpu.SemaphoreType.DMA((2,)),
            pltpu.SemaphoreType.DMA((blocks,)),
            pltpu.SemaphoreType.DMA((n - 1,)),
            pltpu.SemaphoreType.DMA((n - 1,)),
            pltpu.SemaphoreType.DMA((n - 1,)),
            pltpu.SemaphoreType.DMA((n - 1,)),
            pltpu.SemaphoreType.DMA((2, 2, blocks)),
            pltpu.SemaphoreType.DMA((2, 2, blocks)),
        ],
        compiler_params=pltpu.CompilerParams(
            collective_id=0, has_side_effects=True, vmem_limit_bytes=58 * 1024 * 1024
        ),
    )(m, c, rate_kernel, hot, jnp.asarray(tab), jnp.asarray(wind), jnp.asarray(one), spread)
    return out.reshape(count, rows_lat, tile, bins).transpose(0, 2, 1, 3)


def solution(mesh):
    return jax.shard_map(
        shards,
        mesh=mesh,
        in_specs=(
            P("mem", "lon", None, None),
            P("lon", None, "mem"),
            P("lon", None),
            P("lon", None),
            P("lon", None),
            P(),
            P(),
        ),
        out_specs=P("mem", "lon", None, None),
        check_vma=False,
    )
```

time: 207 us -> 67.1 us (0.32)
  waiting for transfers between devices: 108 us -> 0 us
  Pallas kernels: 0 us -> 57.1 us
  matrix products: 29.6 us -> 0 us
  other arithmetic: 24.1 us -> 2.3 us
  local copies, waits for them, and re-layouts: 23.5 us -> 7.32 us
  between operations: 13.6 us -> 0.03 us
  starting transfers between devices: 7.26 us -> 0 us
    all_gather x1 -> x0, waiting for transfers between devices: 66.5 us -> none  [shards(): control_full = lax.all_gather(control, 'mem', axis=2, tiled=True)]
    pallas_call x0 -> x1, Pallas kernels: none -> 57.1 us  [shards(): pl.pallas_call(functools.partial(kernel, n, lons, count, rows_lat, tile,...]
    psum x1 -> x0, waiting for transfers between devices: 34.7 us -> none  [shards(): member_total = lax.psum(local_total, 'mem')]
    dot_general x2 -> x0, matrix products: 29.6 us -> none  [source(): jnp.dot(field.reshape(-1, shape[-1]), kernel, precision=lax.Precision.HIG...]
    mul x10 -> x0, local copies, waits for them, and re-layouts: 15.6 us -> none  [the longest x4 8.19 us: wave_tables(): alignment[..., None] * growth[None, None, None, :]]
    reduce_sum x4 -> x0, other arithmetic: 13.3 us -> none  [the longest x2 8.77 us: source(): energy = jnp.mean(field * field, axis=-1, keepdims=True)]
    ppermute x4 -> x0, starting transfers between devices: 7.18 us -> none  [the longest x2 5.86 us: extended(): after = lax.ppermute(initial, axis, down)]
    ppermute x4 -> x0, waiting for transfers between devices: 6.84 us -> none  [the longest x2 6.83 us: extended(): before = lax.ppermute(last, axis, up)]
  transfers between devices with their start and end apart: 6 -> 0, of which waited for: 4 -> 0; matrix products, arithmetic and copies ran while one was open for 12% -> 0% of each run, Pallas kernels for 0% -> 0%
where the time goes in v1:
time: 67.1 us; the launch traced here: 66.8 us
  Pallas kernels  57.1 us (85%)
  local copies, waits for them, and re-layouts  7.32 us (11%)
  other arithmetic  2.3 us (3%)
    pallas_call x1, Pallas kernels, shards(): pl.pallas_call(functools.partial(kernel, n, lons, count, rows_lat, tile,...  57.1 us
    unnamed x1, local copies, waits for them, and re-layouts  5.05 us

profile of v1, /device:TPU:0, one launch (start us, length us, event | category | flops | bytes accessed | tf_op | source)
XLA Modules:
  0.0 66.8 jit_solution(17149155091779297257)
XLA Ops:
  0.0 0.7 %compare_bitcast_fusion = pred[12,32]{1,0:T(8,128)(4,1)S(1)} fusion(s32[32,12]{0,1:T(8,128)} %param.12), kind=kLoop, calls=%fused_computation.7 | loop fusion | flops 384 | bytes 1920 | tf_op jit(solution)/shard_map/ne | solution.py:345
  0.7 0.1 ne.20
  0.8 0.8 %eq.40 = s32[384]{0:T(512)S(1)} reshape(s32[12,32]{1,0:T(8,128)} %bitcast.17) | data formatting | bytes 3072 | tf_op jit(solution)/shard_map/eq | solution.py:344
  1.6 0.7 %add_bitcast_fusion = s32[12,32]{1,0:T(8,128)S(1)} fusion(s32[32,12]{0,1:T(8,128)} %param.14), kind=kLoop, calls=%fused_computation.6 | loop fusion | flops 384 | bytes 3072 | tf_op jit(solution)/shard_map/add | solution.py:344
  2.3 0.1 add.22
  2.4 0.7 tile.4
  3.0 0.1 tile.10
  3.1 0.6 broadcast_in_dim.14.growth_ref
  3.7 0.9 %fusion.3.oh_ref = f32[384,128]{1,0:T(8,128)} fusion(s32[384]{0:T(512)S(1)} %add.22, s32[384]{0:T(512)S(1)} %eq.40, pred[384]{0:T(512)(128)(4,1)S(1)} %ne.20, pred[128]{0:T(512)(128)(4,1)S(1)} %iota_compare_fusion.2), kind=kLoop, calls=%fused_computation.5 | loop fusion | flops 294912 | bytes 200192 | tf_op jit(solution)/shard_map/jit(_where)/select_n | solution.py:345
  4.6 57.1 %shard_map.100 = f32[4,384,720]{2,1,0:T(8,128)} custom-call(f32[4,384,720]{2,1,0:T(8,128)} %bitcast.15, f32[384,180]{1,0:T(8,128)} %bitcast.16, f32[720,720]{1,0:T(8,128)} %k_hbm.1, f32[384,128]{1,0:T(8,128)} %fusion.3.oh_ref, f32[128,2304]{1,0:T(8,128)} %constant.18.clone.tab_ref, f32[128,768]{1,0:T(8,128)} %constant.19.clone.wind_ref, ...), custom_call_target="tpu_custom_call" | custom-call | tf_op jit(solution)/shard_map/pallas_call | solution.py:354
  61.7 5.1 %copy.12 = f32[4,32,12,720]{3,1,2,0:T(8,128)} copy(f32[4,32,12,720]{3,1,2,0:T(8,128)} %bitcast.14) | data formatting | bytes 8847360
  (2 shorter events, 0.0 us)

commit v2 on v1

--- a/solution.py
+++ b/solution.py
@@ -13,6 +13,7 @@
 FREQS = 30
 LANES = 128
 CLASSES = 4
+SLOTS = 32
 
 
 def round_up(x, to):
@@ -30,22 +31,21 @@
     sin[np.abs(sin) < 1e-9] = 0.0
     lift = lambda v: (v[None, :, None] * speed[:, None, :]).reshape(CLASSES, bins)
     a, b = lift(np.abs(cos)), lift(np.abs(sin))
-    tab = np.zeros((LANES, 3 * width), np.float32)
+    tab = np.zeros((SLOTS, 3 * width), np.float32)
     tab[:CLASSES, :bins] = a
     tab[:CLASSES, width : width + bins] = b
     tab[:CLASSES, 2 * width : 2 * width + bins] = -(a + b)
     tab[CLASSES + DIRS, 2 * width : 2 * width + bins] = 1.0
     rel = np.arange(DIRS)[None, :] - np.arange(DIRS)[:, None]
     align = np.maximum(np.cos(2.0 * math.pi * rel / DIRS), 0.0)
-    wind = np.zeros((LANES, width), np.float32)
+    wind = np.zeros((SLOTS + FREQS + 2, width), np.float32)
     wind[CLASSES : CLASSES + DIRS, :bins] = 0.1 * np.repeat(align, FREQS, axis=1)
-    one = np.zeros((LANES, width), np.float32)
-    one[CLASSES + DIRS, :bins] = 1.0
+    wind[SLOTS : SLOTS + FREQS, :bins] = np.tile(np.eye(FREQS), (1, DIRS))
     cs = np.zeros(width, np.int32)
     sn = np.zeros(width, np.int32)
     cs[:bins] = np.repeat(np.sign(cos), FREQS)
     sn[:bins] = np.repeat(np.sign(sin), FREQS)
-    return tab, wind, one, cs, sn
+    return tab, wind, cs, sn
 
 
 def spans(sign):
@@ -65,9 +65,9 @@
 
 def kernel(
     n, lons, count, rows_lat, tile, bins, width, zspan, mspan, total_members,
-    m_hbm, ctrl_hbm, k_hbm, oh_ref, tab_ref, wind_ref, one_ref, growth_ref,
+    m_hbm, ctrl_hbm, k_hbm, sea_ref, depth_ref, wdir_ref, tab_ref, wind_ref, growth_ref,
     out_hbm,
-    mv, ctrlv, kv, ctrlp, dl, rsb, dfull, f0, f1, ta, tb, tc, tw, rk, lhs, gbuf, ebuf,
+    mv, ctrlv, kv, ctrlp, dl, rsb, dfull, oh_ref, f0, f1, ta, tb, tc, tw, rk, lhs, gbuf, ebuf,
     snd, rcv,
     m_sem, in_sem, out_sem, rs_s, rs_r, ag_s, ag_r, h_s, h_r,
 ):
@@ -76,33 +76,51 @@
     right = lax.rem(at + 1, lons)
     left = lax.rem(at + lons - 1, lons)
     cells = rows_lat * tile
-    part = cells // n
+    quarter = cells // 4
+    bits = n.bit_length() - 1
+    ways = (tuple(range(bits)), tuple(reversed(range(bits))))
     cols = width // LANES
     block = 3 if rows_lat % 3 == 0 else 1
     blocks = rows_lat // block
     own_bins = ctrlv.shape[1]
 
-    def peer(o):
-        return lax.rem(me + o, n)
-
-    def rows_of(q):
-        return pl.ds(pl.multiple_of(q * part, 8), part)
-
-    def m_copy(o):
-        r = rows_of(peer(o))
-        return pltpu.make_async_copy(m_hbm.at[:, r], mv.at[:, r], m_sem.at[o])
-
-    order = list(range(1, n)) + [0]
+    def bit(b):
+        return lax.rem(me // (1 << b), 2)
+
+    def partner(b):
+        return me + (1 - 2 * bit(b)) * (1 << b)
+
+    def rows(start, size):
+        return pl.ds(pl.multiple_of(start, 8), size)
+
+    def kept(h, s):
+        start, size = h * 2 * quarter, 2 * quarter
+        for b in ways[h][:s]:
+            size //= 2
+            start = start + bit(b) * size
+        return start, size
+
+    def given(h, s):
+        start, size = kept(h, s)
+        size //= 2
+        return start + (1 - bit(ways[h][s])) * size, size
+
+    quarters = [given(0, 0)[0], given(1, 0)[0], kept(0, 1)[0], kept(1, 1)[0]]
+
+    def m_copy(q):
+        r = rows(quarters[q], quarter)
+        return pltpu.make_async_copy(m_hbm.at[:, r], mv.at[:, r], m_sem.at[q])
+
     c_copy = pltpu.make_async_copy(ctrl_hbm, ctrlv, in_sem.at[0])
     k_copy = pltpu.make_async_copy(k_hbm, kv, in_sem.at[1])
     c_copy.start()
-    for o in order:
-        m_copy(o).start()
+    for q in range(4):
+        m_copy(q).start()
     k_copy.start()
 
     barrier = pltpu.get_barrier_semaphore()
-    for o in range(1, n):
-        pl.semaphore_signal(barrier, inc=1, device_id={"mem": peer(o)}, device_id_type=pl.DeviceIdType.MESH)
+    for b in range(bits):
+        pl.semaphore_signal(barrier, inc=1, device_id={"mem": partner(b)}, device_id_type=pl.DeviceIdType.MESH)
     for side in (left, right):
         pl.semaphore_signal(barrier, inc=1, device_id={"lon": side}, device_id_type=pl.DeviceIdType.MESH)
 
@@ -113,76 +131,107 @@
         def _():
             ctrlp[:, k * own_bins : (k + 1) * own_bins] = ctrlv[...]
 
-    pl.semaphore_wait(barrier, n + 1)
-
-    def rs_copy(o):
-        q = peer(o)
+    pl.semaphore_wait(barrier, bits + 2)
+
+    def rs_copy(h, s):
+        start, size = given(h, s)
         return pltpu.make_async_remote_copy(
-            src_ref=dl.at[rows_of(q)], dst_ref=rsb.at[o - 1], send_sem=rs_s.at[o - 1], recv_sem=rs_r.at[o - 1],
-            device_id={"mem": q}, device_id_type=pl.DeviceIdType.MESH,
+            src_ref=dl.at[rows(start, size)], dst_ref=rsb.at[h, pl.ds(2 * quarter - 2 * size, size)],
+            send_sem=rs_s.at[h, s], recv_sem=rs_r.at[h, s],
+            device_id={"mem": partner(ways[h][s])}, device_id_type=pl.DeviceIdType.MESH,
         )
 
-    def ag_copy(o):
-        r = rows_of(me)
+    def ag_copy(h, s):
+        r = rows(*kept(h, s + 1))
         return pltpu.make_async_remote_copy(
-            src_ref=dfull.at[r], dst_ref=dfull.at[r], send_sem=ag_s.at[o - 1], recv_sem=ag_r.at[o - 1],
-            device_id={"mem": peer(o)}, device_id_type=pl.DeviceIdType.MESH,
+            src_ref=dfull.at[r], dst_ref=dfull.at[r], send_sem=ag_s.at[h, s], recv_sem=ag_r.at[h, s],
+            device_id={"mem": partner(ways[h][s])}, device_id_type=pl.DeviceIdType.MESH,
         )
 
-    def ag_arrival(o):
-        r = rows_of(lax.rem(me + n - o, n))
+    def ag_arrival(h, s):
+        r = rows(*given(h, s))
         return pltpu.make_async_remote_copy(
-            src_ref=dfull.at[r], dst_ref=dfull.at[r], send_sem=ag_s.at[o - 1], recv_sem=ag_r.at[o - 1],
-            device_id={"mem": peer(o)}, device_id_type=pl.DeviceIdType.MESH,
+            src_ref=dfull.at[r], dst_ref=dfull.at[r], send_sem=ag_s.at[h, s], recv_sem=ag_r.at[h, s],
+            device_id={"mem": partner(ways[h][s])}, device_id_type=pl.DeviceIdType.MESH,
         )
 
-    step = 16 if part % 16 == 0 else 8
-    for o in order:
-        m_copy(o).wait()
-        base = peer(o) * part
-
-        @pl.loop(0, part // step)
+    def local_sum(q):
+        m_copy(q).wait()
+
+        @pl.loop(0, quarter // 16)
         def _(i):
-            r = pl.ds(pl.multiple_of(base + i * step, 8), step)
+            r = rows(quarters[q] + i * 16, 16)
             s = mv[0, r, :]
             for m in range(1, count):
                 s = s + mv[m, r, :]
             dl[r, :] = ctrlp[r, :] - s * (1.0 / total_members)
 
-        if o:
-            rs_copy(o).start()
-
-    @pl.loop(0, rows_lat)
-    def _(i):
-        r = pl.ds(pl.multiple_of(i * tile, 8), tile)
-        oh = oh_ref[r, :]
-        hot = functools.partial(jnp.dot, oh, precision=lax.Precision.HIGHEST, preferred_element_type=jnp.float32)
-        ta[r, :] = hot(tab_ref[:, :width])
-        tb[r, :] = hot(tab_ref[:, width : 2 * width])
-        tc[r, :] = hot(tab_ref[:, 2 * width :])
-        tw[r, :] = hot(wind_ref[...] * growth_ref[...] + one_ref[...])
-
-    rk[...] = jnp.zeros_like(rk)
-    k_copy.wait()
-
-    @pl.loop(0, bins // 16)
-    def _(i):
-        k = kv[pl.ds(pl.multiple_of(i * 16, 16), 16), :] * 0.1
-        hi = k.astype(jnp.bfloat16)
-        lo = (k - hi.astype(jnp.float32)).astype(jnp.bfloat16)
-        rk[pl.ds(pl.multiple_of(i * 16, 16), 16), :bins] = hi
-        rk[pl.ds(pl.multiple_of(width + i * 16, 16), 16), :bins] = hi
-        rk[pl.ds(pl.multiple_of(2 * width + i * 16, 16), 16), :bins] = lo
-
-    zero = jnp.zeros((tile, width), jnp.float32)
-    for m in range(count):
-        for f in (f0, f1):
-            f[m, 0] = zero
-            f[m, rows_lat + 1] = zero
-
-        @pl.loop(0, rows_lat)
+    def take(h, s):
+        rs_copy(h, s).wait_recv()
+        start, size = kept(h, s + 1)
+        to = dl if s < bits - 1 else dfull
+        at_row = 2 * quarter - 2 * size
+
+        @pl.loop(0, size // 8)
         def _(i):
-            f0[m, i + 1, :, width - LANES :] = jnp.zeros((tile, LANES), jnp.float32)
+            r = rows(start + i * 8, 8)
+            to[r, :] = dl[r, :] + rsb[h, rows(at_row + i * 8, 8), :]
+
+    for q in (0, 1):
+        local_sum(q)
+        rs_copy(q, 0).start()
+    for q in (2, 3):
+        local_sum(q)
+
+    slot = lax.broadcasted_iota(jnp.int32, (SLOTS, tile), 0)
+    for i in range(rows_lat):
+        hot = (slot == depth_ref[i : i + 1, :]) | (slot == wdir_ref[i : i + 1, :] + CLASSES) | (slot == CLASSES + DIRS)
+        hot = jnp.where(hot & (sea_ref[i : i + 1, :] != 0), 1.0, 0.0)
+        oh_ref[i * tile : (i + 1) * tile, :] = hot.T
+
+    def split(x):
+        hi = x.astype(jnp.bfloat16)
+        x = x - hi.astype(jnp.float32)
+        mid = x.astype(jnp.bfloat16)
+        return jnp.concatenate([hi, mid, (x - mid.astype(jnp.float32)).astype(jnp.bfloat16)], axis=0)
+
+    spread = jnp.dot(
+        jnp.broadcast_to(growth_ref[...], (8, SLOTS)), wind_ref[SLOTS:, :],
+        precision=lax.Precision.HIGHEST, preferred_element_type=jnp.float32,
+    )
+    slots = lax.broadcasted_iota(jnp.int32, (SLOTS, width), 0)
+    lanes = lax.broadcasted_iota(jnp.int32, (SLOTS, width), 1)
+    gains = wind_ref[:SLOTS, :] * spread[0:1, :]
+    gains = jnp.where((slots == CLASSES + DIRS) & (lanes < bins), 1.0, gains)
+    oh = oh_ref[...].astype(jnp.bfloat16)
+    oh = jnp.concatenate([oh, oh, oh], axis=1)
+    for to, tab in (
+        (ta, tab_ref[:, :width]), (tb, tab_ref[:, width : 2 * width]), (tc, tab_ref[:, 2 * width :]), (tw, gains),
+    ):
+        to[...] = jnp.dot(oh, split(tab), preferred_element_type=jnp.float32)
+
+    def prepare():
+        rk[...] = jnp.zeros_like(rk)
+        k_copy.wait()
+
+        @pl.loop(0, bins // 16)
+        def _(i):
+            k = kv[pl.ds(pl.multiple_of(i * 16, 16), 16), :] * 0.1
+            hi = k.astype(jnp.bfloat16)
+            lo = (k - hi.astype(jnp.float32)).astype(jnp.bfloat16)
+            rk[pl.ds(pl.multiple_of(i * 16, 16), 16), :bins] = hi
+            rk[pl.ds(pl.multiple_of(width + i * 16, 16), 16), :bins] = hi
+            rk[pl.ds(pl.multiple_of(2 * width + i * 16, 16), 16), :bins] = lo
+
+        zero = jnp.zeros((tile, width), jnp.float32)
+        for m in range(count):
+            for f in (f0, f1):
+                f[m, 0] = zero
+                f[m, rows_lat + 1] = zero
+
+            @pl.loop(0, rows_lat)
+            def _(i):
+                f0[m, i + 1, :, width - LANES :] = jnp.zeros((tile, LANES), jnp.float32)
 
     def halo_copies(sub, g):
         r = pl.ds(g * block, block)
@@ -199,20 +248,10 @@
         snd[sub, 0, lat] = jnp.concatenate([f[m, lat + 1, tile - 1 : tile, :] for m in range(count)], axis=0)
         snd[sub, 1, lat] = jnp.concatenate([f[m, lat + 1, 0:1, :] for m in range(count)], axis=0)
 
-    for o in range(1, n):
-        rs_copy(o).wait_recv()
-
-    @pl.loop(0, part // step)
-    def _(i):
-        r = pl.ds(pl.multiple_of(me * part + i * step, 8), step)
-        s = dl[r, :]
-        for o in range(1, n):
-            s = s + rsb[o - 1, pl.ds(pl.multiple_of(i * step, 8), step), :]
-        dfull[r, :] = s
-
-    for o in range(1, n):
-        ag_copy(o).start()
-
+    for s in range(1, bits):
+        for h in (0, 1):
+            take(h, s - 1)
+            rs_copy(h, s).start()
     def recentre(g):
         @pl.loop(0, block)
         def _(i):
@@ -226,16 +265,19 @@
         for c in halo_copies(0, g):
             c.start()
 
-    if blocks == n:
-        for o in range(n):
-            if o:
-                ag_arrival(o).wait_recv()
-            recentre(lax.rem(me + n - o, n))
-    else:
-        for o in range(1, n):
-            ag_arrival(o).wait_recv()
-        for g in range(blocks):
-            recentre(g)
+    prepare()
+    for h in (0, 1):
+        take(h, bits - 1)
+        ag_copy(h, bits - 1).start()
+    for s in reversed(range(bits - 1)):
+        for h in (0, 1):
+            ag_arrival(h, s + 1).wait_recv()
+            ag_copy(h, s).start()
+    for h in (0, 1):
+        recentre(2 * h + bit(ways[h][0]))
+    for h in (0, 1):
+        ag_arrival(h, 0).wait_recv()
+        recentre(2 * h + 1 - bit(ways[h][0]))
 
     row = lax.broadcasted_iota(jnp.int32, (tile, LANES), 0)
     lane = lax.broadcasted_iota(jnp.int32, (tile, LANES), 1)
@@ -314,9 +356,10 @@
     substep(0, f0, to_f1)
     substep(1, f1, to_out)
 
-    for o in range(1, n):
-        rs_copy(o).wait_send()
-        ag_copy(o).wait_send()
+    for h in (0, 1):
+        for s in range(bits):
+            rs_copy(h, s).wait_send()
+            ag_copy(h, s).wait_send()
 
     @pl.loop(0, blocks)
     def _(g):
@@ -331,19 +374,15 @@
     n, lons = lax.axis_size("mem"), lax.axis_size("lon")
     cells = rows_lat * tile
     width = round_up(bins, 2 * LANES)
-    part = cells // n
+    bits = n.bit_length() - 1
+    assert n == 1 << bits and cells % (4 * n) == 0
     block = 3 if rows_lat % 3 == 0 else 1
     blocks = rows_lat // block
-    tab, wind, one, cs, sn = constants(bins, width)
+    tab, wind, cs, sn = constants(bins, width)
 
     m = members.transpose(0, 2, 1, 3).reshape(count, cells, bins)
     c = control.transpose(1, 0, 2).reshape(cells, control.shape[2])
-    flat = lambda x: x.T.reshape(cells, 1)
-    sea, depth, wdir = flat(sea_mask), flat(depth_class), flat(wind_dir)
-    slot = jnp.arange(LANES)[None, :]
-    hot = (slot == depth) | (slot == wdir + CLASSES) | (slot == CLASSES + DIRS)
-    hot = jnp.where(hot & (sea != 0), 1.0, 0.0).astype(jnp.float32)
-    spread = jnp.pad(jnp.tile(growth, DIRS), (0, width - bins))[None]
+    spread = jnp.pad(growth, (0, SLOTS - FREQS))[None]
 
     f32, bf16 = jnp.float32, jnp.bfloat16
     vmem = pl.BlockSpec(memory_space=pltpu.VMEM)
@@ -356,7 +395,7 @@
             kernel, n, lons, count, rows_lat, tile, bins, width, spans(cs), spans(sn), count * n,
         ),
         out_shape=jax.ShapeDtypeStruct((count, cells, bins), f32),
-        in_specs=[hbm, hbm, hbm] + [vmem] * 5,
+        in_specs=[hbm, hbm, hbm] + [vmem] * 6,
         out_specs=hbm,
         scratch_shapes=[
             pltpu.VMEM((count, cells, bins), f32),
@@ -364,8 +403,9 @@
             pltpu.VMEM((bins, bins), f32),
             pltpu.VMEM((cells, bins), f32),
             pltpu.VMEM((cells, bins), f32),
-            pltpu.VMEM((n - 1, part, bins), f32),
+            pltpu.VMEM((2, cells // 2, bins), f32),
             pltpu.VMEM((cells, bins), f32),
+            pltpu.VMEM((cells, SLOTS), f32),
             field, field, table, table, table, table,
             pltpu.VMEM((3 * width, width), bf16),
             pltpu.VMEM((rows, 2 * width), bf16),
@@ -373,20 +413,20 @@
             pltpu.VMEM((rows, LANES), f32),
             pltpu.VMEM((2, 2, rows_lat, count, width), f32),
             pltpu.VMEM((2, 2, rows_lat, count, width), f32),
-            pltpu.SemaphoreType.DMA((n,)),
+            pltpu.SemaphoreType.DMA((4,)),
             pltpu.SemaphoreType.DMA((2,)),
             pltpu.SemaphoreType.DMA((blocks,)),
-            pltpu.SemaphoreType.DMA((n - 1,)),
-            pltpu.SemaphoreType.DMA((n - 1,)),
-            pltpu.SemaphoreType.DMA((n - 1,)),
-            pltpu.SemaphoreType.DMA((n - 1,)),
+            pltpu.SemaphoreType.DMA((2, bits)),
+            pltpu.SemaphoreType.DMA((2, bits)),
+            pltpu.SemaphoreType.DMA((2, bits)),
+            pltpu.SemaphoreType.DMA((2, bits)),
             pltpu.SemaphoreType.DMA((2, 2, blocks)),
             pltpu.SemaphoreType.DMA((2, 2, blocks)),
         ],
         compiler_params=pltpu.CompilerParams(
             collective_id=0, has_side_effects=True, vmem_limit_bytes=58 * 1024 * 1024
         ),
-    )(m, c, rate_kernel, hot, jnp.asarray(tab), jnp.asarray(wind), jnp.asarray(one), spread)
+    )(m, c, rate_kernel, sea_mask.T, depth_class.T, wind_dir.T, jnp.asarray(tab), jnp.asarray(wind), spread)
     return out.reshape(count, rows_lat, tile, bins).transpose(0, 2, 1, 3)
 
 

time: 67.1 us -> 57.4 us (0.86)
  Pallas kernels: 57.1 us -> 50.2 us
  other arithmetic: 2.3 us -> 0 us
  local copies, waits for them, and re-layouts: 7.32 us -> 6.22 us
    pallas_call x1, Pallas kernels: 57.1 us -> 50.2 us  [shards(): pl.pallas_call(functools.partial(kernel, n, lons, count, rows_lat, tile,...]
    select_n x1 -> x0, other arithmetic: 0.9 us -> none  [shards(): hot = jnp.where(hot & (sea != 0), 1.0, 0.0).astype(jnp.float32)]
    eq x1 -> x0, local copies, waits for them, and re-layouts: 0.77 us -> none  [shards(): hot = (slot == depth) | (slot == wdir + CLASSES) | (slot == CLASSES + DIRS)]
    another operation x2 -> x0, local copies, waits for them, and re-layouts: 0.75 us -> none  [shards(): spread = jnp.pad(jnp.tile(growth, DIRS), (0, width - bins))[None]]
    ne x1 -> x0, other arithmetic: 0.7 us -> none  [shards(): hot = jnp.where(hot & (sea != 0), 1.0, 0.0).astype(jnp.float32)]
    add x1 -> x0, other arithmetic: 0.7 us -> none  [shards(): hot = (slot == depth) | (slot == wdir + CLASSES) | (slot == CLASSES + DIRS)]
where the time goes in v2:
time: 57.4 us; the launch traced here: 56.4 us
  Pallas kernels  50.2 us (87%)
  local copies, waits for them, and re-layouts  6.22 us (11%)
    pallas_call x1, Pallas kernels, shards(): pl.pallas_call(functools.partial(kernel, n, lons, count, rows_lat, tile,...  50.2 us
    unnamed x1, local copies, waits for them, and re-layouts  5.05 us
    broadcast_in_dim x1, local copies, waits for them, and re-layouts, shards(): spread = jnp.pad(growth, (0, SLOTS - FREQS))[None]  1.17 us

profile of v2, /device:TPU:0, one launch (start us, length us, event | category | flops | bytes accessed | tf_op | source)
XLA Modules:
  0.0 56.4 jit_solution(13350357470166198777)
XLA Ops:
  0.0 1.2 %pad_bitcast_fusion.growth_ref = f32[1,32]{1,0:T(1,128)} fusion(f32[30]{0:T(128)} %param.14), kind=kLoop, calls=%fused_computation | loop fusion | bytes 248 | tf_op jit(solution)/shard_map/broadcast_in_dim | solution.py:385
  1.2 50.2 %shard_map.91 = f32[4,384,720]{2,1,0:T(8,128)} custom-call(f32[4,384,720]{2,1,0:T(8,128)} %bitcast.15, f32[384,180]{1,0:T(8,128)} %bitcast.16, f32[720,720]{1,0:T(8,128)} %k_hbm.1, s32[12,32]{1,0:T(8,128)} %bitcast.17, s32[12,32]{1,0:T(8,128)} %bitcast.18, s32[12,32]{1,0:T(8,128)} %bitcast.19, f32[32,2304]{1,0:T(8,128)} %constant.7.clone.tab_ref, ...), custom_call_target="tpu_custom_call" | custom-call | tf_op jit(solution)/shard_map/pallas_call | solution.py:393
  51.4 5.1 %copy.11 = f32[4,32,12,720]{3,1,2,0:T(8,128)} copy(f32[4,32,12,720]{3,1,2,0:T(8,128)} %bitcast.14) | data formatting | bytes 8847360

commit v3 on v2

--- a/solution.py
+++ b/solution.py
@@ -67,7 +67,7 @@
     n, lons, count, rows_lat, tile, bins, width, zspan, mspan, total_members,
     m_hbm, ctrl_hbm, k_hbm, sea_ref, depth_ref, wdir_ref, tab_ref, wind_ref, growth_ref,
     out_hbm,
-    mv, ctrlv, kv, ctrlp, dl, rsb, dfull, oh_ref, f0, f1, ta, tb, tc, tw, rk, lhs, gbuf, ebuf,
+    mv, ctrlv, kv, ctrlp, dl, rsb, dfull, oh_ref, f0, f1, ta, tb, tc, tw, rk, lhs, gbuf, ebuf, fd, gm, td,
     snd, rcv,
     m_sem, in_sem, out_sem, rs_s, rs_r, ag_s, ag_r, h_s, h_r,
 ):
@@ -195,8 +195,9 @@
         mid = x.astype(jnp.bfloat16)
         return jnp.concatenate([hi, mid, (x - mid.astype(jnp.float32)).astype(jnp.bfloat16)], axis=0)
 
+    rates = jnp.concatenate([growth_ref[...], jnp.zeros((1, SLOTS - FREQS), jnp.float32)], axis=1)
     spread = jnp.dot(
-        jnp.broadcast_to(growth_ref[...], (8, SLOTS)), wind_ref[SLOTS:, :],
+        jnp.broadcast_to(rates, (8, SLOTS)), wind_ref[SLOTS:, :],
         precision=lax.Precision.HIGHEST, preferred_element_type=jnp.float32,
     )
     slots = lax.broadcasted_iota(jnp.int32, (SLOTS, width), 0)
@@ -223,16 +224,6 @@
             rk[pl.ds(pl.multiple_of(width + i * 16, 16), 16), :bins] = hi
             rk[pl.ds(pl.multiple_of(2 * width + i * 16, 16), 16), :bins] = lo
 
-        zero = jnp.zeros((tile, width), jnp.float32)
-        for m in range(count):
-            for f in (f0, f1):
-                f[m, 0] = zero
-                f[m, rows_lat + 1] = zero
-
-            @pl.loop(0, rows_lat)
-            def _(i):
-                f0[m, i + 1, :, width - LANES :] = jnp.zeros((tile, LANES), jnp.float32)
-
     def halo_copies(sub, g):
         r = pl.ds(g * block, block)
         made = []
@@ -245,39 +236,36 @@
         return made
 
     def keep_edges(sub, f, lat):
-        snd[sub, 0, lat] = jnp.concatenate([f[m, lat + 1, tile - 1 : tile, :] for m in range(count)], axis=0)
-        snd[sub, 1, lat] = jnp.concatenate([f[m, lat + 1, 0:1, :] for m in range(count)], axis=0)
-
-    for s in range(1, bits):
-        for h in (0, 1):
-            take(h, s - 1)
-            rs_copy(h, s).start()
-    def recentre(g):
-        @pl.loop(0, block)
+        picks = range(count) if sub < 2 else [0] * count
+        snd[sub, 0, lat] = jnp.concatenate([f[m, lat + 1, tile - 1 : tile, :] for m in picks], axis=0)
+        snd[sub, 1, lat] = jnp.concatenate([f[m, lat + 1, 0:1, :] for m in picks], axis=0)
+
+    zero = jnp.zeros((tile, width), jnp.float32)
+    for m in range(count):
+        for f in (f0, f1):
+            f[m, 0] = zero
+            f[m, rows_lat + 1] = zero
+
+        @pl.loop(0, rows_lat)
+        def _(i):
+            f0[m, i + 1, :, width - LANES :] = jnp.zeros((tile, LANES), jnp.float32)
+    fd[...] = jnp.zeros_like(fd)
+
+    def recentre(sub, g):
+        @pl.loop(0, block, unroll=True)
         def _(i):
             lat = g * block + i
             r = pl.ds(pl.multiple_of(lat * tile, 8), tile)
             sea = oh_ref[r, CLASSES + DIRS : CLASSES + DIRS + 1] > 0.5
-            d = dfull[r, :]
-            for m in range(count):
-                f0[m, lat + 1, :, :bins] = jnp.where(sea, mv[m, r, :] + d, 0.0)
-            keep_edges(0, f0, lat)
-        for c in halo_copies(0, g):
+            if sub == 0:
+                for m in range(count):
+                    f0[m, lat + 1, :, :bins] = jnp.where(sea, mv[m, r, :], 0.0)
+                keep_edges(0, f0, lat)
+            else:
+                fd[0, lat + 1, :, :bins] = jnp.where(sea, dfull[r, :], 0.0)
+                keep_edges(2, fd, lat)
+        for c in halo_copies(sub, g):
             c.start()
-
-    prepare()
-    for h in (0, 1):
-        take(h, bits - 1)
-        ag_copy(h, bits - 1).start()
-    for s in reversed(range(bits - 1)):
-        for h in (0, 1):
-            ag_arrival(h, s + 1).wait_recv()
-            ag_copy(h, s).start()
-    for h in (0, 1):
-        recentre(2 * h + bit(ways[h][0]))
-    for h in (0, 1):
-        ag_arrival(h, 0).wait_recv()
-        recentre(2 * h + 1 - bit(ways[h][0]))
 
     row = lax.broadcasted_iota(jnp.int32, (tile, LANES), 0)
     lane = lax.broadcasted_iota(jnp.int32, (tile, LANES), 1)
@@ -289,43 +277,124 @@
             return ahead()
         return jnp.where((lane >= span[0]) & (lane < span[1]), behind(), ahead())
 
-    def substep(sub, f, write):
+    def advect(sub, f, lat, many, keep):
+        r = pl.ds(pl.multiple_of(lat * tile, 8), tile)
+        for c in range(cols):
+            l = slice(c * LANES, (c + 1) * LANES)
+            va, vb, vc = ta[r, l], tb[r, l], tc[r, l]
+            for m in range(many):
+                x = f[m, lat + 1, :, l]
+                west = lambda: jnp.where(row == 0, rcv[sub, 0, lat, m : m + 1, l], pltpu.roll(x, 1, 0))
+                east = lambda: jnp.where(row == tile - 1, rcv[sub, 1, lat, m : m + 1, l], pltpu.roll(x, tile - 1, 0))
+                south = lambda: f[m, lat, :, l]
+                north = lambda: f[m, lat + 2, :, l]
+                keep(m, c, l, vc * x + va * pick(zspan[c], west, east) + vb * pick(mspan[c], south, north))
+
+    def stage(q, c, l, v):
+        hi = v.astype(jnp.bfloat16)
+        lhs[q, l] = hi
+        lhs[q, width + c * LANES : width + (c + 1) * LANES] = (v - hi.astype(jnp.float32)).astype(jnp.bfloat16)
+
+    chunk = 2 * LANES
+
+    def product(l, high=None):
+        left_side = jnp.concatenate([lhs[:high], lhs[:high, :width]], axis=1)
+        return jnp.dot(left_side, rk[:, l], preferred_element_type=jnp.float32)
+
+    def members_part(g):
+        for c in halo_copies(0, g):
+            c.wait_recv()
+
+        @pl.loop(0, block, unroll=True)
+        def _(i):
+            lat = g * block + i
+            r = pl.ds(pl.multiple_of(lat * tile, 8), tile)
+
+            def keep(m, c, l, v):
+                gm[m, r, l] = v
+                stage(pl.ds(pl.multiple_of((i * count + m) * tile, 16), tile), c, l, v)
+
+            advect(0, f0, lat, count, keep)
+
+        for c in range(0, width, chunk):
+            l = slice(c, c + chunk)
+            t = product(l)
+            for i in range(block):
+                for m in range(count):
+                    k = (i * count + m) * tile
+                    f1[m, g * block + i + 1, :, l] = t[k : k + tile]
+
+    def difference_part():
         @pl.loop(0, blocks)
         def _(g):
-            for c in halo_copies(sub, g):
+            for c in halo_copies(2, g):
                 c.wait_recv()
 
-            @pl.loop(0, block)
+            @pl.loop(0, block, unroll=True)
             def _(i):
                 lat = g * block + i
-                r = pl.ds(pl.multiple_of(lat * tile, 8), tile)
+                r = pl.ds(pl.multiple_of(lat * tile, 16), tile)
+
+                def keep(m, c, l, v):
+                    gbuf[r, l] = v
+                    stage(r, c, l, v)
+
+                advect(2, fd, lat, 1, keep)
+
+        for c in range(0, width, chunk):
+            l = slice(c, c + chunk)
+            td[:, l] = product(l, cells)
+
+    def join():
+        @pl.loop(0, blocks)
+        def _(g):
+            @pl.loop(0, block, unroll=True)
+            def _(i):
+                lat = g * block + i
+                r = pl.ds(pl.multiple_of(lat * tile, 16), tile)
                 acc = [None] * count
                 for c in range(cols):
                     l = slice(c * LANES, (c + 1) * LANES)
-                    va, vb, vc = ta[r, l], tb[r, l], tc[r, l]
+                    d = gbuf[r, l]
                     for m in range(count):
-                        x = f[m, lat + 1, :, l]
-                        west = lambda: jnp.where(row == 0, rcv[sub, 0, lat, m : m + 1, l], pltpu.roll(x, 1, 0))
-                        east = lambda: jnp.where(row == tile - 1, rcv[sub, 1, lat, m : m + 1, l], pltpu.roll(x, tile - 1, 0))
-                        south = lambda: f[m, lat, :, l]
-                        north = lambda: f[m, lat + 2, :, l]
-                        v = vc * x + va * pick(zspan[c], west, east) + vb * pick(mspan[c], south, north)
+                        v = gm[m, r, l] + d
                         acc[m] = v * v if c == 0 else acc[m] + v * v
-                        q = pl.ds(pl.multiple_of((i * count + m) * tile, 16), tile)
-                        gbuf[q, l] = v
-                        hi = v.astype(jnp.bfloat16)
-                        lhs[q, l] = hi
-                        lhs[q, width + c * LANES : width + (c + 1) * LANES] = (v - hi.astype(jnp.float32)).astype(jnp.bfloat16)
+                e = [jnp.broadcast_to(jnp.sum(a, axis=1, keepdims=True) * (0.05 / bins), (tile, LANES)) for a in acc]
+                for c in range(cols):
+                    l = slice(c * LANES, (c + 1) * LANES)
+                    d, w, t = gbuf[r, l], tw[r, l], td[r, l]
+                    for m in range(count):
+                        f1[m, lat + 1, :, l] = (gm[m, r, l] + d) * (w - e[m]) + (f1[m, lat + 1, :, l] + t)
+                keep_edges(1, f1, lat)
+            for c in halo_copies(1, g):
+                c.start()
+
+    def last_substep():
+        @pl.loop(0, blocks)
+        def _(g):
+            for c in halo_copies(1, g):
+                c.wait_recv()
+
+            @pl.loop(0, block, unroll=True)
+            def _(i):
+                lat = g * block + i
+                acc = [None] * count
+
+                def keep(m, c, l, v):
+                    acc[m] = v * v if c == 0 else acc[m] + v * v
+                    q = pl.ds(pl.multiple_of((i * count + m) * tile, 16), tile)
+                    gbuf[q, l] = v
+                    stage(q, c, l, v)
+
+                advect(1, f1, lat, count, keep)
                 for m in range(count):
                     q = pl.ds(pl.multiple_of((i * count + m) * tile, 16), tile)
                     e = jnp.sum(acc[m], axis=1, keepdims=True) * (0.05 / bins)
                     ebuf[q, :] = jnp.broadcast_to(e, (tile, LANES))
 
-            chunk = 2 * LANES
             for c in range(0, width, chunk):
                 l = slice(c, c + chunk)
-                left_side = jnp.concatenate([lhs[...], lhs[:, :width]], axis=1)
-                t = jnp.dot(left_side, rk[:, l], preferred_element_type=jnp.float32)
+                t = product(l)
                 for i in range(block):
                     lat = g * block + i
                     w = tw[pl.ds(pl.multiple_of(lat * tile, 8), tile), l]
@@ -333,28 +402,48 @@
                         k = (i * count + m) * tile
                         e = ebuf[k : k + tile, :]
                         e = jnp.concatenate([e] * (chunk // LANES), axis=1)
-                        write(m, lat, l, gbuf[k : k + tile, l] * (w - e) + t[k : k + tile])
-            if sub == 0:
-                for i in range(block):
-                    keep_edges(1, f1, g * block + i)
-                for c in halo_copies(1, g):
-                    c.start()
-            else:
-                out_copy(g).start()
+                        to_out(m, lat, l, gbuf[k : k + tile, l] * (w - e) + t[k : k + tile])
+            out_copy(g).start()
+
+    work = [lambda g=g: members_part(g) for g in range(blocks)]
+    for g in range(blocks):
+        recentre(0, g)
+    for s in range(1, bits):
+        for h in (0, 1):
+            take(h, s - 1)
+            rs_copy(h, s).start()
+        if s == 1:
+            prepare()
+        if work:
+            work.pop(0)()
+    for h in (0, 1):
+        take(h, bits - 1)
+        ag_copy(h, bits - 1).start()
+    for s in reversed(range(bits - 1)):
+        if work:
+            work.pop(0)()
+        for h in (0, 1):
+            ag_arrival(h, s + 1).wait_recv()
+            ag_copy(h, s).start()
+    for h in (0, 1):
+        recentre(2, 2 * h + bit(ways[h][0]))
+    for w in work:
+        w()
+    for h in (0, 1):
+        ag_arrival(h, 0).wait_recv()
+        recentre(2, 2 * h + 1 - bit(ways[h][0]))
 
     def out_copy(g):
         r = pl.ds(pl.multiple_of(g * block * tile, 8), block * tile)
         return pltpu.make_async_copy(mv.at[:, r], out_hbm.at[:, r], out_sem.at[g])
 
-    def to_f1(m, lat, l, v):
-        f1[m, lat + 1, :, l] = v
-
     def to_out(m, lat, l, v):
         stop = min(l.stop, bins)
         mv[m, pl.ds(pl.multiple_of(lat * tile, 8), tile), l.start : stop] = v[:, : stop - l.start]
 
-    substep(0, f0, to_f1)
-    substep(1, f1, to_out)
+    difference_part()
+    join()
+    last_substep()
 
     for h in (0, 1):
         for s in range(bits):
@@ -363,7 +452,7 @@
 
     @pl.loop(0, blocks)
     def _(g):
-        for sub in range(2):
+        for sub in range(3):
             for c in halo_copies(sub, g):
                 c.wait_send()
         out_copy(g).wait()
@@ -382,7 +471,7 @@
 
     m = members.transpose(0, 2, 1, 3).reshape(count, cells, bins)
     c = control.transpose(1, 0, 2).reshape(cells, control.shape[2])
-    spread = jnp.pad(growth, (0, SLOTS - FREQS))[None]
+    spread = growth[None]
 
     f32, bf16 = jnp.float32, jnp.bfloat16
     vmem = pl.BlockSpec(memory_space=pltpu.VMEM)
@@ -390,6 +479,7 @@
     field = pltpu.VMEM((count, rows_lat + 2, tile, width), f32)
     table = pltpu.VMEM((cells, width), f32)
     rows = block * count * tile
+    assert rows >= cells
     out = pl.pallas_call(
         functools.partial(
             kernel, n, lons, count, rows_lat, tile, bins, width, spans(cs), spans(sn), count * n,
@@ -411,8 +501,11 @@
             pltpu.VMEM((rows, 2 * width), bf16),
             pltpu.VMEM((rows, width), f32),
             pltpu.VMEM((rows, LANES), f32),
-            pltpu.VMEM((2, 2, rows_lat, count, width), f32),
-            pltpu.VMEM((2, 2, rows_lat, count, width), f32),
+            pltpu.VMEM((1, rows_lat + 2, tile, width), f32),
+            pltpu.VMEM((count, cells, width), f32),
+            table,
+            pltpu.VMEM((3, 2, rows_lat, count, width), f32),
+            pltpu.VMEM((3, 2, rows_lat, count, width), f32),
             pltpu.SemaphoreType.DMA((4,)),
             pltpu.SemaphoreType.DMA((2,)),
             pltpu.SemaphoreType.DMA((blocks,)),
@@ -420,8 +513,8 @@
             pltpu.SemaphoreType.DMA((2, bits)),
             pltpu.SemaphoreType.DMA((2, bits)),
             pltpu.SemaphoreType.DMA((2, bits)),
-            pltpu.SemaphoreType.DMA((2, 2, blocks)),
-            pltpu.SemaphoreType.DMA((2, 2, blocks)),
+            pltpu.SemaphoreType.DMA((3, 2, blocks)),
+            pltpu.SemaphoreType.DMA((3, 2, blocks)),
         ],
         compiler_params=pltpu.CompilerParams(
             collective_id=0, has_side_effects=True, vmem_limit_bytes=58 * 1024 * 1024

time: 57.4 us -> 54.3 us (0.946); the launches traced: 56.4 us -> 54.2 us
  local copies, waits for them, and re-layouts: 6.22 us -> 5.05 us
  Pallas kernels: 50.2 us -> 49.1 us
    broadcast_in_dim x1 -> x0, local copies, waits for them, and re-layouts: 1.17 us -> none  [shards(): spread = jnp.pad(growth, (0, SLOTS - FREQS))[None]]
    pallas_call x1, Pallas kernels: 50.2 us -> 49.1 us  [shards(): pl.pallas_call(functools.partial(kernel, n, lons, count, rows_lat, tile,...]
where the time goes in v3:
time: 54.3 us; the launch traced here: 54.2 us
  Pallas kernels  49.1 us (90%)
  local copies, waits for them, and re-layouts  5.05 us (9%)
    pallas_call x1, Pallas kernels, shards(): pl.pallas_call(functools.partial(kernel, n, lons, count, rows_lat, tile,...  49.1 us
    unnamed x1, local copies, waits for them, and re-layouts  5.05 us

profile of v3, /device:TPU:0, one launch (start us, length us, event | category | flops | bytes accessed | tf_op | source)
XLA Modules:
  0.0 54.2 jit_solution(4374321008712273285)
XLA Ops:
  0.0 49.1 %shard_map.91 = f32[4,384,720]{2,1,0:T(8,128)} custom-call(f32[4,384,720]{2,1,0:T(8,128)} %bitcast.14, f32[384,180]{1,0:T(8,128)} %bitcast.15, f32[720,720]{1,0:T(8,128)} %k_hbm.1, s32[12,32]{1,0:T(8,128)} %bitcast.16, s32[12,32]{1,0:T(8,128)} %bitcast.17, s32[12,32]{1,0:T(8,128)} %bitcast.18, f32[32,2304]{1,0:T(8,128)} %constant.4.clone.tab_ref, ...), custom_call_target="tpu_custom_call" | custom-call | tf_op jit(solution)/shard_map/pallas_call | solution.py:483
  49.1 5.1 %copy.11 = f32[4,32,12,720]{3,1,2,0:T(8,128)} copy(f32[4,32,12,720]{3,1,2,0:T(8,128)} %bitcast.13) | data formatting | bytes 8847360
